TPU v7x, 128 devices: a whole 4x4x4 slice. The times are simulated.
128 devices in a mesh: tsnk: 8 (over y, z_hi), tsrc: 16 (over x, z_lo, core).
Axes of the slice: x: 4, y: 4, z: 4 (z_hi: 2, z_lo: 2; z = z_hi * 2 + z_lo), core: 2. Of those that a mesh axis runs over, the one named last changes fastest.
Arguments:
- perambulator: bfloat16 [16, 16, 2, 384, 384], P('tsnk', 'tsrc'), may hold values from -0.5 to 0.5
- elementals: bfloat16 [16, 2, 2, 384, 384], P('tsrc'), may hold values from -0.5 to 0.5
- op_mom: int32 [4, 2], replicated, may hold values from 0 to 1
Outputs:
- correlators: float32 [16, 16, 3, 2, 4, 4], P('tsnk', 'tsrc')
All inputs are finite; a program needn't handle non-finite values.
Results may differ from a plain program's by a relative error of at most 0.0067.
Values may be sent and summed in bfloat16 or wider, within the bound.
A program may use at most 128 MiB of HBM per device.

v0:
```python
import jax
import jax.numpy as jnp
from jax import lax
from jax.sharding import PartitionSpec as P


def from_root(shard, axis, root):
    mine = lax.axis_index(axis) == root
    return lax.psum(jnp.where(mine, shard, jnp.zeros_like(shard)), axis)


def cmul(left, right):
    real_part = jnp.dot(left[0], right[0], preferred_element_type=jnp.float32) - jnp.dot(
        left[1], right[1], preferred_element_type=jnp.float32
    )
    imag_part = jnp.dot(left[0], right[1], preferred_element_type=jnp.float32) + jnp.dot(
        left[1], right[0], preferred_element_type=jnp.float32
    )
    return jnp.stack([real_part, imag_part]).astype(jnp.bfloat16)


def dagger(block):
    return jnp.stack([block[0].T, -block[1].T])


def trace_table(first, second):
    count = first.shape[0]
    other = second.shape[0]
    width = first.shape[-1] * first.shape[-1]
    flat_a = first.reshape(count, 2, width)
    flat_b = jnp.swapaxes(second, -1, -2).reshape(other, 2, width)

    def inner(u, v):
        return lax.dot_general(
            flat_a[:, u], flat_b[:, v], (((1,), (1,)), ((), ())), preferred_element_type=jnp.float32
        )

    real_part = inner(0, 0) - inner(1, 1)
    imag_part = inner(0, 1) + inner(1, 0)
    return jnp.stack([real_part, imag_part])


def pair_correlators(forward, sink_el, source_el, diag_snk, diag_src, op_mom):
    moms = sink_el.shape[0]
    backward = dagger(forward)
    q_list = [cmul(source_el[m], backward) for m in range(moms)]
    x_list = [cmul(forward, q_list[m]) for m in range(moms)]
    g_list = [cmul(forward, source_el[m]) for m in range(moms)]
    r_list = [cmul(diag_src, q_list[m]) for m in range(moms)]
    s_list = [cmul(sink_el[m], diag_snk) for m in range(moms)]
    l_arr = jnp.stack([cmul(sink_el[a], g_list[m]) for a in range(moms) for m in range(moms)])
    p_arr = jnp.stack([cmul(sink_el[a], x_list[m]) for a in range(moms) for m in range(moms)])
    m_arr = jnp.stack([cmul(r_list[m], s_list[a]) for m in range(moms) for a in range(moms)])
    box = trace_table(p_arr, p_arr).reshape(2, moms, moms, moms, moms)
    rect = trace_table(l_arr, m_arr).reshape(2, moms, moms, moms, moms)
    tri = trace_table(l_arr, jnp.stack(r_list)).reshape(2, moms, moms, moms)
    one_a = op_mom[:, 0][:, None]
    two_a = op_mom[:, 1][:, None]
    one_b = op_mom[:, 0][None, :]
    two_b = op_mom[:, 1][None, :]
    box_out = box[:, one_a, one_b, two_a, two_b]
    rect_out = rect[:, one_a, one_b, two_b, two_a]
    tri_out = tri[:, one_a, one_b, two_b]
    return jnp.stack([box_out, rect_out, tri_out])


def on_device(perambulator, elementals, op_mom):
    sinks = perambulator.shape[0]
    sink_row = lax.axis_index("tsnk")
    source_col = lax.axis_index("tsrc")
    own_source = elementals[0]
    slot = source_col % sinks
    own_diag = lax.dynamic_index_in_dim(perambulator[:, 0], slot, 0, keepdims=False)
    diag_src = from_root(own_diag, "tsnk", source_col // sinks)
    every_time = lax.all_gather(elementals, "tsrc", axis=0, tiled=True)
    outputs = []
    for local in range(sinks):
        root = sink_row * sinks + local
        sink_el = lax.dynamic_index_in_dim(every_time, root, 0, keepdims=False)
        diag_snk = from_root(perambulator[local, 0], "tsrc", root)
        outputs.append(
            pair_correlators(
                perambulator[local, 0], sink_el, own_source, diag_snk, diag_src, op_mom
            )
        )
    return jnp.stack(outputs)[:, None]


def solution(mesh):
    placed = (P("tsnk", "tsrc", None, None, None), P("tsrc", None, None, None, None), P())
    return jax.shard_map(
        on_device,
        mesh=mesh,
        in_specs=placed,
        out_specs=P("tsnk", "tsrc", None, None, None, None),
        check_vma=False,
    )
```

profile of v0, /device:TPU:1, one launch (start us, length us, event | category | flops | bytes accessed | tf_op | source)
XLA Modules:
  0.0 663.3 jit_solution(6179139880891162309)
XLA Ops:
  6.5 2.7 select_bitcast_fusion.1
  30.4 2.1 fusion.20
  46.7 2.1 fusion.65
  48.8 2.2 fusion.64
  51.0 2.2 fusion.61
  62.1 31.7 %all-reduce.4.cloned.1.call-done = bf16[2,384,384]{2,1,0:T(8,128)(2,1)} async-done(((bf16[2,384,384]{2,1,0:T(8,128)(2,1)}), bf16[2,384,384]{2,1,0:T(8,128)(2,1)}) %all-reduce.4.cloned.1.call-update) | async-done | bytes 589840 | tf_op jit(solution)/shard_map/psum | solution.py:9
  99.8 2.4 copy.104
  103.7 2.7 fusion.416
  109.6 1.5 copy.132
  112.5 2.9 fusion.417
  115.5 104.5 %all-reduce.6.cloned.1.call-done = (bf16[2,384,384]{2,1,0:T(8,128)(2,1)}, bf16[2,384,384]{2,1,0:T(8,128)(2,1)}) async-done(((bf16[2,384,384]{2,1,0:T(8,128)(2,1)}, bf16[2,384,384]{2,1,0:T(8,128)(2,1)}), (bf16[2,384,384]{2,1,0:T(8,128)(2,1)}, bf16[2,384,384]{2,1,0:T(8,128)(2,1)})) %all-reduce.6.cloned.1.call-update) | async-done | bytes 1179664 | tf_op jit(solution)/shard_map/psum | solution.py:9
  220.0 104.7 %all-gather.2.cloned.1.call-done = bf16[16,2,2,384,384]{4,3,2,1,0:T(8,128)(2,1)} async-done(((bf16[1,2,2,384,384]{4,3,2,1,0:T(8,128)(2,1)}), bf16[16,2,2,384,384]{4,3,2,1,0:T(8,128)(2,1)}) %all-gather.2.cloned.1.call-update) | async-done | bytes 18874384 | tf_op jit(solution)/shard_map/all_gather | solution.py:75
  378.9 3.1 copy.100
  382.0 2.7 reshape.1424
  384.8 4.4 fusion.413
  389.2 6.1 maximum_maximum_fusion.1
  395.3 2.8 fusion.104
  398.1 2.8 fusion.106
  429.8 1.9 maximum_bitcast_fusion
  431.7 2.6 copy.88
  434.3 2.7 reshape.1423
  437.1 4.3 fusion.412
  441.5 6.2 maximum_maximum_fusion
  447.8 2.8 fusion.112
  450.6 2.7 fusion.114
  474.5 2.0 fusion.71
  479.0 2.0 fusion.70
  481.0 1.9 stack.663
  484.2 2.0 fusion.69
  486.2 1.9 stack.661
  489.4 2.0 fusion.68
  491.4 1.9 stack.660
  494.7 2.0 fusion.67
  496.7 1.9 stack.658
  503.5 2.0 fusion.63
  505.5 2.3 stack.655
  518.0 2.6 copy.128
  520.6 2.7 reshape.1427
  523.4 4.4 fusion.415
  527.8 6.1 maximum_maximum_fusion.3
  533.9 2.8 fusion.88
  536.7 2.7 fusion.90
  568.3 1.6 maximum_bitcast_fusion.2
  569.8 2.6 copy.116
  572.5 2.7 reshape.1426
  575.2 4.4 fusion.414
  579.7 6.2 maximum_maximum_fusion.2
  585.9 2.8 fusion.96
  588.7 2.8 fusion.98
  591.6 1.7 fusion.160
  593.3 2.3 fusion.161
  598.1 2.9 convolution_subtract_fusion.45
  602.7 3.3 fusion.145
  606.1 3.9 fusion.142
  611.5 4.0 fusion.139
  616.2 4.5 fusion.136
  623.6 3.1 fusion.162
  626.7 2.3 fusion.163
  629.0 1.6 convolution_add_fusion.44
  633.3 2.9 convolution_subtract_fusion.44
  638.5 3.3 fusion.157
  641.8 3.9 fusion.154
  646.7 4.0 fusion.151
  650.8 3.9 fusion.148
  (510 shorter events, 226.3 us)
Async XLA Ops:
  6.5 87.3 %all-reduce.4.cloned.1.call-start = ((), (), s32[]{:S(2)}) async-start(), calls=%async_computation.1 | async-start | bytes 1179648 | tf_op jit(solution)/shard_map/psum | solution.py:9
  9.3 210.7 %all-reduce.6.cloned.1.call-start = ((), (), s32[]{:S(2)}) async-start(), calls=%async_computation.2 | async-start | bytes 2359296 | tf_op jit(solution)/shard_map/psum | solution.py:9
  10.1 314.6 %all-gather.2.cloned.1.call-start = ((), (), s32[]{:S(2)}) async-start(), calls=%async_computation | async-start | bytes 20054016 | tf_op jit(solution)/shard_map/all_gather | solution.py:75
  14.8 4.8 copy-start.120
  25.3 4.7 copy-start.113
  48.8 5.4 copy-start.103
  55.4 5.7 copy-start.35
  59.9 35.3 %copy-start.33 = (bf16[384,384]{1,0:T(8,128)(2,1)S(1)}, bf16[384,384]{1,0:T(8,128)(2,1)}, u32[]{:S(2)}) copy-start(bf16[384,384]{1,0:T(8,128)(2,1)} %fusion.6) | copy-start | bytes 884740
  61.0 35.9 %copy-start.30 = (bf16[384,384]{1,0:T(8,128)(2,1)S(1)}, bf16[384,384]{1,0:T(8,128)(2,1)}, u32[]{:S(2)}) copy-start(bf16[384,384]{1,0:T(8,128)(2,1)} %fusion) | copy-start | bytes 884740
  62.1 35.1 %copy-start.34 = (bf16[384,384]{1,0:T(8,128)(2,1)S(1)}, bf16[384,384]{1,0:T(8,128)(2,1)}, u32[]{:S(2)}) copy-start(bf16[384,384]{1,0:T(8,128)(2,1)} %fusion.6) | copy-start | bytes 884740
  115.4 212.1 %copy-start.4 = (bf16[384,384]{1,0:T(8,128)(2,1)S(1)}, bf16[384,384]{1,0:T(8,128)(2,1)}, u32[]{:S(2)}) copy-start(bf16[384,384]{1,0:T(8,128)(2,1)} %copy-done.3) | copy-start | bytes 884740
  115.4 213.2 %copy-start.6 = (bf16[384,384]{1,0:T(8,128)(2,1)S(1)}, bf16[384,384]{1,0:T(8,128)(2,1)}, u32[]{:S(2)}) copy-start(bf16[384,384]{1,0:T(8,128)(2,1)} %copy-done.5) | copy-start | bytes 884740
  324.7 5.2 copy-start.8
  341.0 5.0 copy-start.22
  348.3 4.9 copy-start.21
  368.6 4.6 copy-start.26
  370.9 5.3 copy-start.28
  384.7 4.5 copy-start.55
  384.7 4.5 copy-start.56
  384.7 4.4 copy-start.58
  384.7 4.4 copy-start.60
  384.7 4.4 copy-start.62
  384.7 4.4 copy-start.64
  384.8 4.4 copy-start.66
  384.8 4.4 copy-start.71
  403.6 5.9 copy-start.43
  403.6 4.6 copy-start.17
  404.5 4.9 copy-start.19
  407.2 5.9 copy-start.44
  410.8 5.9 copy-start.45
  414.4 5.9 copy-start.46
  418.0 5.9 copy-start.48
  421.6 5.8 copy-start.50
  425.2 4.6 copy-start.52
  437.0 4.4 copy-start.69
  437.0 4.4 copy-start.72
  437.0 4.4 copy-start.75
  468.1 5.1 copy-start.15
  469.5 5.0 copy-start.16
  476.5 6.4 copy-start.13
  477.6 6.6 copy-start.14
  511.3 4.4 copy-start.109
  523.3 4.4 copy-start.57
  523.3 4.4 copy-start.59
  523.3 4.4 copy-start.61
  523.3 4.4 copy-start.63
  523.4 4.4 copy-start.65
  523.4 4.4 copy-start.67
  523.4 4.4 copy-start.73
  542.1 4.6 copy-start.9
  543.1 4.9 copy-start.11
  556.5 5.9 copy-start.47
  560.1 5.9 copy-start.49
  563.7 4.5 copy-start.51
  575.2 4.4 copy-start.68
  575.2 4.4 copy-start.70
  575.2 4.4 copy-start.74
  575.2 4.4 copy-start.76
  606.1 5.4 copy-start.127
  611.5 4.7 copy-start.89
  616.2 7.3 %copy-start.114 = (bf16[2,1,147456]{2,1,0:T(2,128)(2,1)S(1)}, bf16[2,1,147456]{2,1,0:T(2,128)(2,1)}, u32[]{:S(2)}) copy-start(bf16[2,1,147456]{2,1,0:T(2,128)(2,1)} %get-tuple-element.21) | copy-start | bytes 1769476
  641.8 4.8 copy-start.130
  650.8 4.9 copy-start.118
  650.8 4.9 copy-start.119
  (70 other events, 196.9 us)
Sparse Core Ops, SparseCore 0:
  9.8 83.9 all-reduce.3
  96.4 123.5 all-reduce.5
  221.7 102.9 all-gather.1
where the time goes:
time: 676 us; the launch traced here: 663 us
  matrix products  266 us (39%)
  waiting for transfers between devices  242 us (36%)
  local copies, waits for them, and re-layouts  102 us (15%)
  other arithmetic  36.8 us (5%)
  between operations  16 us (2%)
    psum x2, waiting for transfers between devices, from_root(): return lax.psum(jnp.where(mine, shard, jnp.zeros_like(shard)), axis)  136 us
    all_gather x1, waiting for transfers between devices, on_device(): every_time = lax.all_gather(elementals, 'tsrc', axis=0, tiled=True)  105 us
    dot_general x24, matrix products, inner(): lax.dot_general(flat_a[:, u], flat_b[:, v], (((1,), (1,)), ((), ())), pre...  71 us
    dot_general x44, matrix products, cmul(): jnp.dot(left[1], right[0], preferred_element_type=jnp.float32)  49.7 us
    dot_general x44, matrix products, cmul(): jnp.dot(left[0], right[0], preferred_element_type=jnp.float32)  49.1 us
    dot_general x44, matrix products, cmul(): jnp.dot(left[0], right[1], preferred_element_type=jnp.float32)  48.7 us
    dot_general x44, matrix products, cmul(): jnp.dot(left[1], right[1], preferred_element_type=jnp.float32)  47.8 us
    another operation x32, local copies, waits for them, and re-layouts, cmul(): return jnp.stack([real_part, imag_part]).astype(jnp.bfloat16)  35.4 us
  transfers between devices with their start and end apart: 3, of which 3 were waited for; matrix products, arithmetic and copies ran while one was open for 11% of the time, Pallas kernels for 0%

commit v1 on v0

v1 whole, which is shorter than its diff:
```python
import jax
import jax.numpy as jnp
from jax import lax
from jax.experimental import pallas as pl
from jax.experimental.pallas import tpu as pltpu
from jax.sharding import PartitionSpec as P

N = 384
W = 2 * N
BF = jnp.bfloat16
NN = (((1,), (0,)), ((), ()))
NT = (((1,), (1,)), ((), ()))
MESH = pl.DeviceIdType.MESH


def wait_for(ref, sem):
    pltpu.make_async_copy(ref, ref, sem).wait()


class Gather:
    def __init__(self, buf, place, device, send_sem, recv_sem):
        self.buf, self.send_sem, self.recv_sem = buf, send_sem, recv_sem
        a, b = place // 2, place % 2
        self.other = device(a * 2 + 1 - b)
        self.right = device(lax.rem(a + 1, 4) * 2 + b)
        self.left = device(lax.rem(a + 3, 4) * 2 + b)
        self.a, self.b = a, b
        self.sent = []

    def slot(self, step, flip):
        b = 1 - self.b if flip else self.b
        return lax.rem(self.a + step, 4) * 2 + b

    def send(self, slot, to):
        n = len(self.sent)
        copy = pltpu.make_async_remote_copy(
            src_ref=self.buf.at[slot], dst_ref=self.buf.at[slot], send_sem=self.send_sem.at[n],
            recv_sem=self.recv_sem.at[slot], device_id=to, device_id_type=MESH)
        copy.start()
        self.sent.append(copy)

    def wait(self, slot):
        wait_for(self.buf.at[slot], self.recv_sem.at[slot])

    def own(self):
        mine = self.slot(0, False)
        self.wait(mine)
        for to in (self.other, self.right, self.left):
            self.send(mine, to)

    def pair(self):
        slot = self.slot(0, True)
        self.wait(slot)
        for to in (self.right, self.left):
            self.send(slot, to)

    def sides(self):
        for step in (3, 1):
            for flip in (False, True):
                self.wait(self.slot(step, flip))
        self.send(self.slot(3, False), self.right)
        self.send(self.slot(1, True), self.left)

    def last(self):
        for flip in (False, True):
            self.wait(self.slot(2, flip))

    def drain(self):
        for copy in self.sent:
            copy.wait_send()


def rows(r, i):
    return jnp.concatenate([r, i], axis=1)


def block(r, i):
    return jnp.concatenate([rows(r, i), rows(-i, r)], axis=0)


def block_t(r, i):
    return jnp.concatenate([rows(r, -i), rows(i, r)], axis=0)


def mul(left, right, dims=NN):
    return lax.dot_general(left, right, dims, preferred_element_type=jnp.float32).astype(BF)


def exact(left, right):
    return lax.dot_general(
        left, right, NN, precision=lax.Precision.HIGHEST, preferred_element_type=jnp.float32)


def halves(ref):
    return ref[:, :N], ref[:, N:]


def parts(ref):
    count, depth = ref.shape[0] // 2, ref.shape[1]
    return ref[:count].reshape(count * depth, N), ref[count:].reshape(count * depth, N)


def elemental(ref, m):
    return parts(ref.at[pl.ds(4 * m, 4)])


def two(ref, s):
    return jnp.concatenate([ref[s, 0], ref[s, 1]], axis=0)


def forward_products(f, psi, g):
    def body(b, _):
        left = jnp.concatenate([rows(*parts(f.at[s])) for s in range(2)], axis=0)
        out = mul(left, block(*elemental(psi, b)))
        g[0, b] = out[:N]
        g[1, b] = out[N:]
        return 0
    lax.fori_loop(0, 2, body, 0)


def back_products(f, psi, q):
    def body(s, _):
        left = jnp.concatenate([rows(*elemental(psi, b)) for b in range(2)], axis=0)
        out = mul(left, block(*parts(f.at[s])), NT)
        q[s, 0] = out[:N]
        q[s, 1] = out[N:]
        return 0
    lax.fori_loop(0, 2, body, 0)


def from_left(left, s, q, out):
    def body(b, _):
        out[s, b] = mul(rows(*parts(left)), block(*halves(q.at[s, b])))
        return 0
    lax.fori_loop(0, 2, body, 0)


def loop_products(s, g, r, y):
    def body(b, _):
        out = mul(two(g, s), block(*halves(r.at[s, b])))
        y[s, b] = out[:N]
        y[s, 2 + b] = out[N:]
        return 0
    lax.fori_loop(0, 2, body, 0)


def box_products(s, phi, x, p, pt):
    def body(b, _):
        left = jnp.concatenate([rows(*elemental(phi.at[s], a)) for a in range(2)], axis=0)
        out = mul(left, block(*halves(x.at[s, b])))
        for a in range(2):
            part = out[a * N:(a + 1) * N]
            p[s, 2 * a + b] = part
            pt[s, 2 * a + b] = rows(part[:, :N].T, part[:, N:].T)
        return 0
    lax.fori_loop(0, 2, body, 0)


def sink_transposes(s, phi, phit):
    def body(a, _):
        r, i = elemental(phi.at[s], a)
        phit[s, a] = rows(r.T, i.T)
        return 0
    lax.fori_loop(0, 2, body, 0)


def sink_products(s, phi, phit, df, st, zt):
    left = jnp.concatenate([rows(*elemental(phi.at[s], a)) for a in range(2)], axis=0)
    out = mul(left, block(*parts(df)))
    st[0] = out[:N]
    st[1] = out[N:]

    def second(a, _):
        out = mul(two(phit, s), block_t(*halves(st.at[a])), NT)
        zt[s, 2 * a] = out[:N]
        zt[s, 2 * a + 1] = out[N:]
        return 0
    lax.fori_loop(0, 2, second, 0)


def grouped(refs):
    out = []
    for ref in refs:
        for c in range(2):
            out.append(jnp.concatenate(
                [ref[32 * k:32 * k + 32, c * N:(c + 1) * N] for k in range(N // 32)], axis=1))
    return jnp.concatenate(out, axis=0)


def iotas(shape):
    return lax.broadcasted_iota(jnp.int32, shape, 0), lax.broadcasted_iota(jnp.int32, shape, 1)


def diagonal(left, right):
    acc = lax.dot_general(grouped(left), grouped(right), NT, preferred_element_type=jnp.float32)
    r, c = iotas(acc.shape)
    kept = jnp.where(r % 32 == c % 32, acc, 0.0)
    return jnp.sum(kept.reshape(acc.shape[0] // 32, 32, acc.shape[1]), axis=1)


def chosen(op, which, index):
    out = jnp.zeros(index.shape, jnp.int32)
    for p in range(4):
        out = jnp.where(index == p, op[which, p], out)
    return out


def as_f32(mask):
    return jnp.where(mask, 1.0, 0.0).astype(jnp.float32)


def put(out, s, k, table):
    out[s, 0, k, 0] = table[0:4, 0:4] - table[4:8, 4:8]
    out[s, 0, k, 1] = table[0:4, 4:8] + table[4:8, 0:4]


def box_traces(s, op, p, pt, out):
    acc = diagonal([p.at[s, k] for k in range(4)], [pt.at[s, k] for k in range(4)])
    r, c = iotas((16, 8))
    pick = (r // 8 == (c // 2) % 2) & ((r // 4) % 2 == c % 2) & (chosen(op, 0, r % 4) == c // 4)
    half = exact(as_f32(pick), acc)
    r, c = iotas((256, 16))
    pick = (r // 128 == c // 8) & ((r // 32) % 2 == (c // 4) % 2) & (chosen(op, 1, c % 4) == (r // 64) % 2)
    full = exact(half, as_f32(pick))
    r, c = iotas((16, 16))
    keep = (chosen(op, 0, c % 4) == r // 8) & (chosen(op, 1, r % 4) == c // 8)
    full = jnp.where(keep, full, 0.0)
    full = full[0:8] + full[8:16]
    put(out, s, 0, full[:, 0:8] + full[:, 8:16])


def loop_traces(s, op, zt, phit, y, out):
    acc = diagonal(
        [zt.at[s, k] for k in range(4)] + [phit.at[s, a] for a in range(2)], [y.at[s, k] for k in range(4)])
    acc = jnp.concatenate([acc, jnp.zeros((4, 256), jnp.float32)], axis=0)
    r, c = iotas((256, 8))
    pick = ((r // 32) % 2 == c // 4) & (chosen(op, 0, c % 4) == r // 128) & (chosen(op, 1, c % 4) == (r // 64) % 2)
    half = exact(acc, as_f32(pick))
    r, c = iotas((16, 16))
    rect = (r < 8) & (c < 8) & (c // 4 == chosen(op, 1, r % 4)) & ((c // 2) % 2 == chosen(op, 0, r % 4))
    tri = (r >= 8) & (c >= 8) & ((c - 8) // 2 == chosen(op, 0, r % 4))
    pick = (rect | tri) & ((r // 4) % 2 == c % 2)
    full = exact(as_f32(pick), half)
    put(out, s, 1, full[0:8])
    put(out, s, 2, full[8:16])


def kernel(op, f, psi, out, phi, df, di, g, x, q, r, y, p, pt, phit, st, zt,
           phi_send, phi_recv, df_send, df_recv, di_send, di_recv, swap_send, root_send,
           twin_send, twin_recv, z_send, z_recv):
    j = lax.axis_index("tsnk")
    column = lax.axis_index("tsrc")
    k, c = column // 2, column % 2
    twin = 1 - c
    swapped = (k, 2 * j + c)
    sibling = (j, 2 * k + twin)

    def in_row(q):
        return (j, 2 * q + c)

    def in_column(q):
        return (q, 2 * k + c)

    phi_ring = Gather(phi.at[c], k, in_row, phi_send, phi_recv)
    df_ring = Gather(df, k, in_row, df_send, df_recv)
    di_ring = Gather(di, j, in_column, di_send, di_recv)

    barrier = pltpu.get_barrier_semaphore()

    def greet(to):
        pl.semaphore_signal(barrier, inc=1, device_id=to, device_id_type=MESH)

    for to in (sibling, di_ring.other, di_ring.right, di_ring.left, phi_ring.other, phi_ring.right, phi_ring.left):
        greet(to)

    def mates(do):
        for q in range(8):
            @pl.when(q != j)
            def _():
                do(q)

    @pl.when(j == k)
    def _():
        def both(q):
            greet(in_row(q))
            greet(in_column(q))
        mates(both)
        pl.semaphore_wait(barrier, 21)

    @pl.when(j != k)
    def _():
        greet(swapped)
        greet((j, 2 * j + c))
        greet((k, 2 * k + c))
        pl.semaphore_wait(barrier, 10)

    def scatter(q, buf, sems, n, to):
        return pltpu.make_async_remote_copy(
            src_ref=f.at[c, q], dst_ref=buf.at[q], send_sem=root_send.at[8 * n + q], recv_sem=sems.at[q],
            device_id=to, device_id_type=MESH)

    def swap():
        return pltpu.make_async_remote_copy(
            src_ref=psi.at[j], dst_ref=phi.at[c, j], send_sem=swap_send, recv_sem=phi_recv.at[j],
            device_id=swapped, device_id_type=MESH)

    @pl.when(j == k)
    def _():
        pltpu.make_async_copy(f.at[c, j], di.at[j], di_recv.at[j]).start()
        mates(lambda q: scatter(q, di, di_recv, 0, in_column(q)).start())
        pltpu.make_async_copy(psi.at[j], phi.at[c, j], phi_recv.at[j]).start()
        pltpu.make_async_copy(f.at[c, j], df.at[j], df_recv.at[j]).start()
        mates(lambda q: scatter(q, df, df_recv, 1, in_row(q)).start())

    @pl.when(j != k)
    def _():
        swap().start()

    to_twin = []

    def share(step):
        a = lax.rem(k // 2 + step, 4)
        piece = phi.at[c, pl.ds(2 * a, 2)]
        copy = pltpu.make_async_remote_copy(
            src_ref=piece, dst_ref=piece, send_sem=twin_send.at[a], recv_sem=twin_recv.at[a],
            device_id=sibling, device_id_type=MESH)
        copy.start()
        to_twin.append(copy)

    forward_products(f, psi, g)
    di_ring.own()
    back_products(f, psi, q)
    di_ring.pair()
    phi_ring.own()
    from_left(f.at[0], 0, q, x)
    di_ring.sides()
    phi_ring.pair()
    share(0)
    from_left(f.at[1], 1, q, x)
    di_ring.last()
    from_left(di, 0, q, r)
    phi_ring.sides()
    share(3)
    share(1)
    from_left(di, 1, q, r)
    df_ring.own()
    phi_ring.last()
    share(2)
    loop_products(0, g, r, y)
    df_ring.pair()
    loop_products(1, g, r, y)
    df_ring.sides()
    box_products(c, phi, x, p, pt)
    sink_transposes(c, phi, phit)
    df_ring.last()
    sink_products(c, phi, phit, df, st, zt)
    z_copy = pltpu.make_async_remote_copy(
        src_ref=zt.at[c], dst_ref=zt.at[c], send_sem=z_send, recv_sem=z_recv, device_id=sibling, device_id_type=MESH)
    z_copy.start()
    box_traces(c, op, p, pt, out)
    for a in range(4):
        wait_for(phi.at[twin, pl.ds(2 * a, 2)], twin_recv.at[a])
    box_products(twin, phi, x, p, pt)
    sink_transposes(twin, phi, phit)
    box_traces(twin, op, p, pt, out)
    loop_traces(c, op, zt, phit, y, out)
    wait_for(zt.at[twin], z_recv)
    loop_traces(twin, op, zt, phit, y, out)

    for ring in (di_ring, phi_ring, df_ring):
        ring.drain()
    for copy in to_twin + [z_copy]:
        copy.wait_send()

    @pl.when(j == k)
    def _():
        mates(lambda q: scatter(q, di, di_recv, 0, in_column(q)).wait_send())
        mates(lambda q: scatter(q, df, df_recv, 1, in_row(q)).wait_send())

    @pl.when(j != k)
    def _():
        swap().wait_send()


def on_device(perambulator, elementals, op_mom):
    f = perambulator.reshape(2, 8, 2 * N // 8, N)
    psi = elementals.reshape(8, 4 * N // 8, N)
    vmem = pl.BlockSpec(memory_space=pltpu.VMEM)
    sems = pltpu.SemaphoreType.DMA
    return pl.pallas_call(
        kernel,
        out_shape=jax.ShapeDtypeStruct((2, 1, 3, 2, 4, 4), jnp.float32),
        in_specs=[pl.BlockSpec(memory_space=pltpu.SMEM), vmem, vmem],
        out_specs=vmem,
        scratch_shapes=[
            pltpu.VMEM((2, 8, 4 * N // 8, N), BF),
            pltpu.VMEM((8, 2 * N // 8, N), BF),
            pltpu.VMEM((8, 2 * N // 8, N), BF),
            pltpu.VMEM((2, 2, N, W), BF),
            pltpu.VMEM((2, 2, N, W), BF),
            pltpu.VMEM((2, 2, N, W), BF),
            pltpu.VMEM((2, 2, N, W), BF),
            pltpu.VMEM((2, 4, N, W), BF),
            pltpu.VMEM((2, 4, N, W), BF),
            pltpu.VMEM((2, 4, N, W), BF),
            pltpu.VMEM((2, 2, N, W), BF),
            pltpu.VMEM((2, N, W), BF),
            pltpu.VMEM((2, 4, N, W), BF),
            sems((7,)), sems((8,)), sems((7,)), sems((8,)), sems((7,)), sems((8,)),
            sems, sems((16,)), sems((4,)), sems((4,)), sems, sems,
        ],
        compiler_params=pltpu.CompilerParams(
            collective_id=0, has_side_effects=True, vmem_limit_bytes=60 * 2**20),
        cost_estimate=pl.CostEstimate(flops=20_000_000_000, bytes_accessed=4_000_000, transcendentals=0),
    )(op_mom.T, f, psi)


def solution(mesh):
    placed = (P("tsnk", "tsrc", None, None, None), P("tsrc", None, None, None, None), P())
    return jax.shard_map(
        on_device,
        mesh=mesh,
        in_specs=placed,
        out_specs=P("tsnk", "tsrc", None, None, None, None),
        check_vma=False,
    )
```

time: 676 us -> 68.7 us (0.10)
  the two profiles are of different devices: /device:TPU:1 before, /device:TPU:0 now
where the time goes in v1:
time: 68.7 us; the launch traced here: 68.5 us
  Pallas kernels  67.2 us (98%)
  local copies, waits for them, and re-layouts  1.35 us (2%)
    pallas_call x1, Pallas kernels, on_device(): pl.pallas_call(kernel, out_shape=jax.ShapeDtypeStruct((2, 1, 3, 2, 4, 4),...  67.2 us

profile of v1, /device:TPU:0, one launch (start us, length us, event | category | flops | bytes accessed | tf_op | source)
XLA Modules:
  0.0 68.5 jit_solution(14003231730262193852)
XLA Ops:
  0.0 67.2 %shard_map.37 = f32[2,1,3,2,4,4]{5,4,3,2,1,0:T(4,128)} custom-call(s32[2,4]{1,0:T(2,128)} %bitcast.5, bf16[2,8,96,384]{3,2,1,0:T(8,128)(2,1)} %bitcast.3, bf16[8,192,384]{2,1,0:T(8,128)(2,1)} %bitcast.4), custom_call_target="tpu_custom_call" | custom-call | flops 20000000000 | bytes 4000000 | tf_op jit(solution)/shard_map/pallas_call | solution.py:390
  67.2 1.3 %copy.5 = f32[2,1,3,2,4,4]{5,4,3,2,1,0:T(4,128)} copy(f32[2,1,3,2,4,4]{5,4,3,2,1,0:T(4,128)} %shard_map.37) | data formatting | bytes 1536

commit v2 on v1

v2 whole, which is shorter than its diff:
```python
import jax
import jax.numpy as jnp
from jax import lax
from jax.experimental import pallas as pl
from jax.experimental.pallas import tpu as pltpu
from jax.sharding import PartitionSpec as P

N = 384
W = 2 * N
BF = jnp.bfloat16
NN = (((1,), (0,)), ((), ()))
NT = (((1,), (1,)), ((), ()))
MESH = pl.DeviceIdType.MESH


def wait_for(ref, sem):
    pltpu.make_async_copy(ref, ref, sem).wait()


def rows(r, i):
    return jnp.concatenate([r, i], axis=1)


def block(r, i):
    return jnp.concatenate([rows(r, i), rows(-i, r)], axis=0)


def block_t(r, i):
    return jnp.concatenate([rows(r, -i), rows(i, r)], axis=0)


def mul(left, right, dims=NN):
    return lax.dot_general(left, right, dims, preferred_element_type=jnp.float32).astype(BF)


def exact(left, right):
    return lax.dot_general(
        left, right, NN, precision=lax.Precision.HIGHEST, preferred_element_type=jnp.float32)


def halves(ref):
    return ref[:, :N], ref[:, N:]


def parts(ref):
    count, depth = ref.shape[0] // 2, ref.shape[1]
    return ref[:count].reshape(count * depth, N), ref[count:].reshape(count * depth, N)


def two(ref, s):
    return jnp.concatenate([ref[s, 0], ref[s, 1]], axis=0)


def forward_products(f, psi, g):
    def body(b, _):
        left = jnp.concatenate([rows(*parts(f.at[s])) for s in range(2)], axis=0)
        out = mul(left, block(*parts(psi.at[b])))
        g[0, b] = out[:N]
        g[1, b] = out[N:]
        return 0
    lax.fori_loop(0, 2, body, 0)


def back_products(f, psi, q):
    def body(s, _):
        left = jnp.concatenate([rows(*parts(psi.at[b])) for b in range(2)], axis=0)
        out = mul(left, block(*parts(f.at[s])), NT)
        q[s, 0] = out[:N]
        q[s, 1] = out[N:]
        return 0
    lax.fori_loop(0, 2, body, 0)


def from_left(left, s, q, out):
    def body(b, _):
        out[s, b] = mul(rows(*parts(left)), block(*halves(q.at[s, b])))
        return 0
    lax.fori_loop(0, 2, body, 0)


def loop_products(s, g, r, y):
    def body(b, _):
        out = mul(two(g, s), block(*halves(r.at[s, b])))
        y[s, b] = out[:N]
        y[s, 2 + b] = out[N:]
        return 0
    lax.fori_loop(0, 2, body, 0)


def box_products(s, a, phi, x, p, pt):
    def body(b, _):
        out = mul(rows(*parts(phi.at[s, a])), block(*halves(x.at[s, b])))
        p[s, 2 * a + b] = out
        pt[s, 2 * a + b] = rows(out[:, :N].T, out[:, N:].T)
        return 0
    lax.fori_loop(0, 2, body, 0)


def sink_transposes(s, phi, phit):
    def body(a, _):
        r, i = parts(phi.at[s, a])
        phit[s, a] = rows(r.T, i.T)
        return 0
    lax.fori_loop(0, 2, body, 0)


def sink_products(s, phi, phit, df, st, zt):
    left = jnp.concatenate([rows(*parts(phi.at[s, a])) for a in range(2)], axis=0)
    out = mul(left, block(*parts(df)))
    st[0] = out[:N]
    st[1] = out[N:]

    def second(a, _):
        out = mul(two(phit, s), block_t(*halves(st.at[a])), NT)
        zt[s, 2 * a] = out[:N]
        zt[s, 2 * a + 1] = out[N:]
        return 0
    lax.fori_loop(0, 2, second, 0)


def grouped(refs):
    out = []
    for ref in refs:
        for c in range(2):
            out.append(jnp.concatenate(
                [ref[32 * k:32 * k + 32, c * N:(c + 1) * N] for k in range(N // 32)], axis=1))
    return jnp.concatenate(out, axis=0)


def iotas(shape):
    return lax.broadcasted_iota(jnp.int32, shape, 0), lax.broadcasted_iota(jnp.int32, shape, 1)


def diagonal(left, right):
    acc = lax.dot_general(grouped(left), grouped(right), NT, preferred_element_type=jnp.float32)
    r, c = iotas(acc.shape)
    kept = jnp.where(r % 32 == c % 32, acc, 0.0)
    return jnp.sum(kept.reshape(acc.shape[0] // 32, 32, acc.shape[1]), axis=1)


def chosen(op, which, index):
    out = jnp.zeros(index.shape, jnp.int32)
    for p in range(4):
        out = jnp.where(index == p, op[which, p], out)
    return out


def as_f32(mask):
    return jnp.where(mask, 1.0, 0.0).astype(jnp.float32)


def put(out, s, k, table):
    out[s, 0, k, 0] = table[0:4, 0:4] - table[4:8, 4:8]
    out[s, 0, k, 1] = table[0:4, 4:8] + table[4:8, 0:4]


def box_traces(s, op, p, pt, out):
    acc = diagonal([p.at[s, k] for k in range(4)], [pt.at[s, k] for k in range(4)])
    r, c = iotas((16, 8))
    pick = (r // 8 == (c // 2) % 2) & ((r // 4) % 2 == c % 2) & (chosen(op, 0, r % 4) == c // 4)
    half = exact(as_f32(pick), acc)
    r, c = iotas((256, 16))
    pick = (r // 128 == c // 8) & ((r // 32) % 2 == (c // 4) % 2) & (chosen(op, 1, c % 4) == (r // 64) % 2)
    full = exact(half, as_f32(pick))
    r, c = iotas((16, 16))
    keep = (chosen(op, 0, c % 4) == r // 8) & (chosen(op, 1, r % 4) == c // 8)
    full = jnp.where(keep, full, 0.0)
    full = full[0:8] + full[8:16]
    put(out, s, 0, full[:, 0:8] + full[:, 8:16])


def loop_traces(s, op, zt, phit, y, out):
    acc = diagonal(
        [zt.at[s, k] for k in range(4)] + [phit.at[s, a] for a in range(2)], [y.at[s, k] for k in range(4)])
    acc = jnp.concatenate([acc, jnp.zeros((4, 256), jnp.float32)], axis=0)
    r, c = iotas((256, 8))
    pick = ((r // 32) % 2 == c // 4) & (chosen(op, 0, c % 4) == r // 128) & (chosen(op, 1, c % 4) == (r // 64) % 2)
    half = exact(acc, as_f32(pick))
    r, c = iotas((16, 16))
    rect = (r < 8) & (c < 8) & (c // 4 == chosen(op, 1, r % 4)) & ((c // 2) % 2 == chosen(op, 0, r % 4))
    tri = (r >= 8) & (c >= 8) & ((c - 8) // 2 == chosen(op, 0, r % 4))
    pick = (rect | tri) & ((r // 4) % 2 == c % 2)
    full = exact(as_f32(pick), half)
    put(out, s, 1, full[0:8])
    put(out, s, 2, full[8:16])


def kernel(op, f_hbm, psi_hbm, out, f, psi, phi, df, di, g, x, q, r, y, p, pt, phit, st, zt,
           phi_send, phi_recv, df_send, df_recv, di_send, di_recv, root_send,
           twin_send, twin_recv, z_send, z_recv, load_sem):
    j = lax.axis_index("tsnk")
    column = lax.axis_index("tsrc")
    k, c = column // 2, column % 2
    twin = 1 - c
    sibling = (j, 2 * k + twin)

    def later(place, step):
        return lax.rem(place + step, 8)

    def remote(src, dst, send, recv, to):
        return pltpu.make_async_remote_copy(
            src_ref=src, dst_ref=dst, send_sem=send, recv_sem=recv, device_id=to, device_id_type=MESH)

    loads = [pltpu.make_async_copy(psi_hbm, psi, load_sem.at[0]), pltpu.make_async_copy(f_hbm, f, load_sem.at[1])]
    for copy in loads:
        copy.start()

    barrier = pltpu.get_barrier_semaphore()

    def greet(to):
        pl.semaphore_signal(barrier, inc=1, device_id=to, device_id_type=MESH)

    greet(sibling)
    for step in range(1, 8):
        greet((j, 2 * later(k, step) + c))
        greet((later(j, step), column))
        greet((later(j, step), 2 * j + c))

    @pl.when(j != k)
    def _():
        greet((j, 2 * j + c))
        pl.semaphore_wait(barrier, 23)

    @pl.when(j == k)
    def _():
        pl.semaphore_wait(barrier, 22)

    def scatter():
        out = []
        for step in range(1, 8):
            n = later(j, step)
            out.append(remote(f_hbm.at[c, n], di.at[n], root_send.at[step], di_recv.at[n], (n, column)))
        for step in range(1, 8):
            n = later(k, step)
            out.append(remote(f_hbm.at[c, n], df.at[n], root_send.at[7 + step], df_recv.at[n], (j, 2 * n + c)))
        return out

    def sinks(a, step):
        return remote(psi_hbm.at[a, j], phi.at[c, a, j], phi_send.at[a, step], phi_recv.at[a, j],
                      (k, 2 * later(k, step) + c))

    def along_column(step):
        return remote(di.at[j], di.at[j], di_send.at[step], di_recv.at[j], (later(j, step), column))

    def along_row(step):
        return remote(df.at[k], df.at[k], df_send.at[step], df_recv.at[k], (j, 2 * later(k, step) + c))

    def send_elementals(a):
        for step in range(1, 8):
            sinks(a, step).start()

        @pl.when(j != k)
        def _():
            sinks(a, 0).start()

        @pl.when(j == k)
        def _():
            pltpu.make_async_copy(psi_hbm.at[a, j], phi.at[c, a, j], phi_recv.at[a, j]).start()

    def send_pieces(buf, sems, own, along):
        wait_for(buf.at[own], sems.at[own])
        for step in range(1, 8):
            along(step).start()

    def receive(buf, sems, own):
        for step in range(1, 8):
            n = later(own, step)
            wait_for(buf.at[n], sems.at[n])

    def share(a):
        return remote(phi.at[c, a], phi.at[c, a], twin_send.at[a], twin_recv.at[a], sibling)

    def receive_elementals(a):
        for n in range(8):
            wait_for(phi.at[c, a, n], phi_recv.at[a, n])
        share(a).start()

    def receive_shared(a):
        wait_for(phi.at[twin, a], twin_recv.at[a])

    @pl.when(j == k)
    def _():
        for copy in scatter():
            copy.start()
        pltpu.make_async_copy(f_hbm.at[c, j], di.at[j], di_recv.at[j]).start()
        pltpu.make_async_copy(f_hbm.at[c, j], df.at[j], df_recv.at[j]).start()

    send_elementals(0)
    for copy in loads:
        copy.wait()
    forward_products(f, psi, g)
    back_products(f, psi, q)
    send_pieces(di, di_recv, j, along_column)
    send_elementals(1)
    from_left(f.at[0], 0, q, x)
    send_pieces(df, df_recv, k, along_row)
    from_left(f.at[1], 1, q, x)
    receive_elementals(0)
    box_products(c, 0, phi, x, p, pt)
    receive_shared(0)
    box_products(twin, 0, phi, x, p, pt)
    receive(di, di_recv, j)
    from_left(di, 0, q, r)
    from_left(di, 1, q, r)
    loop_products(0, g, r, y)
    receive_elementals(1)
    loop_products(1, g, r, y)
    box_products(c, 1, phi, x, p, pt)
    sink_transposes(c, phi, phit)
    receive(df, df_recv, k)
    sink_products(c, phi, phit, df, st, zt)
    z_copy = remote(zt.at[c], zt.at[c], z_send, z_recv, sibling)
    z_copy.start()
    receive_shared(1)
    box_products(twin, 1, phi, x, p, pt)
    sink_transposes(twin, phi, phit)
    box_traces(c, op, p, pt, out)
    box_traces(twin, op, p, pt, out)
    loop_traces(c, op, zt, phit, y, out)
    wait_for(zt.at[twin], z_recv)
    loop_traces(twin, op, zt, phit, y, out)

    for step in range(1, 8):
        for copy in (sinks(0, step), sinks(1, step), along_column(step), along_row(step)):
            copy.wait_send()
    for copy in (share(0), share(1), z_copy):
        copy.wait_send()

    @pl.when(j == k)
    def _():
        for copy in scatter():
            copy.wait_send()

    @pl.when(j != k)
    def _():
        for a in range(2):
            sinks(a, 0).wait_send()


def on_device(perambulator, elementals, op_mom):
    piece = 2 * N // 8
    anywhere = pl.BlockSpec(memory_space=pl.ANY)
    sems = pltpu.SemaphoreType.DMA
    return pl.pallas_call(
        kernel,
        out_shape=jax.ShapeDtypeStruct((2, 1, 3, 2, 4, 4), jnp.float32),
        in_specs=[pl.BlockSpec(memory_space=pltpu.SMEM), anywhere, anywhere],
        out_specs=pl.BlockSpec(memory_space=pltpu.VMEM),
        scratch_shapes=[
            pltpu.VMEM((2, 8, piece, N), BF),
            pltpu.VMEM((2, 8, piece, N), BF),
            pltpu.VMEM((2, 2, 8, piece, N), BF),
            pltpu.VMEM((8, piece, N), BF),
            pltpu.VMEM((8, piece, N), BF),
            pltpu.VMEM((2, 2, N, W), BF),
            pltpu.VMEM((2, 2, N, W), BF),
            pltpu.VMEM((2, 2, N, W), BF),
            pltpu.VMEM((2, 2, N, W), BF),
            pltpu.VMEM((2, 4, N, W), BF),
            pltpu.VMEM((2, 4, N, W), BF),
            pltpu.VMEM((2, 4, N, W), BF),
            pltpu.VMEM((2, 2, N, W), BF),
            pltpu.VMEM((2, N, W), BF),
            pltpu.VMEM((2, 4, N, W), BF),
            sems((2, 8)), sems((2, 8)), sems((8,)), sems((8,)), sems((8,)), sems((8,)), sems((16,)),
            sems((2,)), sems((2,)), sems, sems, sems((2,)),
        ],
        compiler_params=pltpu.CompilerParams(
            collective_id=0, has_side_effects=True, vmem_limit_bytes=60 * 2**20),
        cost_estimate=pl.CostEstimate(flops=20_000_000_000, bytes_accessed=4_000_000, transcendentals=0),
    )(op_mom.T, perambulator.reshape(2, 8, piece, N), elementals.reshape(2, 8, piece, N))


def solution(mesh):
    placed = (P("tsnk", "tsrc", None, None, None), P("tsrc", None, None, None, None), P())
    return jax.shard_map(
        on_device,
        mesh=mesh,
        in_specs=placed,
        out_specs=P("tsnk", "tsrc", None, None, None, None),
        check_vma=False,
    )
```

time: 68.7 us -> 65.3 us (0.951)
  the two profiles are of different devices: /device:TPU:0 before, /device:TPU:22 now
where the time goes in v2:
time: 65.3 us; the launch traced here: 65.1 us
  Pallas kernels  63.7 us (98%)
  local copies, waits for them, and re-layouts  1.35 us (2%)
    pallas_call x1, Pallas kernels, on_device(): pl.pallas_call(kernel, out_shape=jax.ShapeDtypeStruct((2, 1, 3, 2, 4, 4),...  63.7 us
    unnamed x1, local copies, waits for them, and re-layouts  1.35 us

profile of v2, /device:TPU:22, one launch (start us, length us, event | category | flops | bytes accessed | tf_op | source)
XLA Modules:
  0.0 65.1 jit_solution(12686678263130258214)
XLA Ops:
  0.0 63.7 %shard_map.37 = f32[2,1,3,2,4,4]{5,4,3,2,1,0:T(4,128)} custom-call(s32[2,4]{1,0:T(2,128)} %bitcast.5, bf16[2,8,96,384]{3,2,1,0:T(8,128)(2,1)} %bitcast.3, bf16[2,8,96,384]{3,2,1,0:T(8,128)(2,1)} %bitcast.4), custom_call_target="tpu_custom_call" | custom-call | flops 20000000000 | bytes 4000000 | tf_op jit(solution)/shard_map/pallas_call | solution.py:344
  63.7 1.3 %copy.5 = f32[2,1,3,2,4,4]{5,4,3,2,1,0:T(4,128)} copy(f32[2,1,3,2,4,4]{5,4,3,2,1,0:T(4,128)} %shard_map.37) | data formatting | bytes 1536

commit v3 on v2

--- a/solution.py
+++ b/solution.py
@@ -52,70 +52,71 @@
 
 
 def forward_products(f, psi, g):
-    def body(b, _):
+    def body(b):
         left = jnp.concatenate([rows(*parts(f.at[s])) for s in range(2)], axis=0)
         out = mul(left, block(*parts(psi.at[b])))
         g[0, b] = out[:N]
         g[1, b] = out[N:]
-        return 0
-    lax.fori_loop(0, 2, body, 0)
+    for n in range(2):
+        body(n)
 
 
 def back_products(f, psi, q):
-    def body(s, _):
+    def body(s):
         left = jnp.concatenate([rows(*parts(psi.at[b])) for b in range(2)], axis=0)
         out = mul(left, block(*parts(f.at[s])), NT)
         q[s, 0] = out[:N]
         q[s, 1] = out[N:]
-        return 0
-    lax.fori_loop(0, 2, body, 0)
+    for n in range(2):
+        body(n)
 
 
 def from_left(left, s, q, out):
-    def body(b, _):
+    def body(b):
         out[s, b] = mul(rows(*parts(left)), block(*halves(q.at[s, b])))
-        return 0
-    lax.fori_loop(0, 2, body, 0)
+    for n in range(2):
+        body(n)
 
 
 def loop_products(s, g, r, y):
-    def body(b, _):
+    def body(b):
         out = mul(two(g, s), block(*halves(r.at[s, b])))
         y[s, b] = out[:N]
         y[s, 2 + b] = out[N:]
-        return 0
-    lax.fori_loop(0, 2, body, 0)
+    for n in range(2):
+        body(n)
 
 
 def box_products(s, a, phi, x, p, pt):
-    def body(b, _):
+    def body(b):
         out = mul(rows(*parts(phi.at[s, a])), block(*halves(x.at[s, b])))
         p[s, 2 * a + b] = out
         pt[s, 2 * a + b] = rows(out[:, :N].T, out[:, N:].T)
-        return 0
-    lax.fori_loop(0, 2, body, 0)
+    for n in range(2):
+        body(n)
 
 
 def sink_transposes(s, phi, phit):
-    def body(a, _):
+    def body(a):
         r, i = parts(phi.at[s, a])
         phit[s, a] = rows(r.T, i.T)
-        return 0
-    lax.fori_loop(0, 2, body, 0)
-
-
-def sink_products(s, phi, phit, df, st, zt):
+    for n in range(2):
+        body(n)
+
+
+def sink_products(s, phi, phit, df, st, zt, done):
     left = jnp.concatenate([rows(*parts(phi.at[s, a])) for a in range(2)], axis=0)
     out = mul(left, block(*parts(df)))
     st[0] = out[:N]
     st[1] = out[N:]
 
-    def second(a, _):
+    def second(a):
         out = mul(two(phit, s), block_t(*halves(st.at[a])), NT)
         zt[s, 2 * a] = out[:N]
         zt[s, 2 * a + 1] = out[N:]
-        return 0
-    lax.fori_loop(0, 2, second, 0)
+        done(a)
+    for n in range(2):
+        second(n)
 
 
 def grouped(refs):
@@ -186,7 +187,7 @@
 
 
 def kernel(op, f_hbm, psi_hbm, out, f, psi, phi, df, di, g, x, q, r, y, p, pt, phit, st, zt,
-           phi_send, phi_recv, df_send, df_recv, di_send, di_recv, root_send,
+           phi_send, phi_recv, df_recv, di_recv, push_send, root_send,
            twin_send, twin_recv, z_send, z_recv, load_sem):
     j = lax.axis_index("tsnk")
     column = lax.axis_index("tsrc")
@@ -239,11 +240,42 @@
         return remote(psi_hbm.at[a, j], phi.at[c, a, j], phi_send.at[a, step], phi_recv.at[a, j],
                       (k, 2 * later(k, step) + c))
 
-    def along_column(step):
-        return remote(di.at[j], di.at[j], di_send.at[step], di_recv.at[j], (later(j, step), column))
-
-    def along_row(step):
-        return remote(df.at[k], df.at[k], df_send.at[step], df_recv.at[k], (j, 2 * later(k, step) + c))
+    def across(place, step):
+        return lax.rem(place // 2 + step, 4) * 2 + lax.rem(place, 2)
+
+    def pair(place):
+        return place + 1 - 2 * lax.rem(place, 2)
+
+    sent = []
+
+    def push(buf, sems, slot, to):
+        copy = remote(buf.at[slot], buf.at[slot], push_send.at[len(sent)], sems.at[slot], to)
+        copy.start()
+        sent.append(copy)
+
+    def in_row(place):
+        return (j, 2 * place + c)
+
+    def in_column(place):
+        return (place, column)
+
+    def arrive(buf, sems, slot):
+        wait_for(buf.at[slot], sems.at[slot])
+
+    def spread(buf, sems, own, slot, where):
+        arrive(buf, sems, slot)
+        for step in (1, 3, 2):
+            push(buf, sems, slot, where(across(own, step)))
+
+    def spread_and_pair(buf, sems, own, where):
+        spread(buf, sems, own, own, where)
+        push(buf, sems, own, where(pair(own)))
+
+    def pass_on(buf, sems, own, where):
+        for step in (1, 3, 2):
+            slot = across(own, step)
+            arrive(buf, sems, slot)
+            push(buf, sems, slot, where(pair(own)))
 
     def send_elementals(a):
         for step in range(1, 8):
@@ -257,15 +289,9 @@
         def _():
             pltpu.make_async_copy(psi_hbm.at[a, j], phi.at[c, a, j], phi_recv.at[a, j]).start()
 
-    def send_pieces(buf, sems, own, along):
-        wait_for(buf.at[own], sems.at[own])
-        for step in range(1, 8):
-            along(step).start()
-
-    def receive(buf, sems, own):
-        for step in range(1, 8):
-            n = later(own, step)
-            wait_for(buf.at[n], sems.at[n])
+    def hand(a):
+        piece = zt.at[c, pl.ds(2 * a, 2)]
+        return remote(piece, piece, z_send.at[a], z_recv.at[a], sibling)
 
     def share(a):
         return remote(phi.at[c, a], phi.at[c, a], twin_send.at[a], twin_recv.at[a], sibling)
@@ -286,44 +312,49 @@
         pltpu.make_async_copy(f_hbm.at[c, j], df.at[j], df_recv.at[j]).start()
 
     send_elementals(0)
+    send_elementals(1)
     for copy in loads:
         copy.wait()
     forward_products(f, psi, g)
     back_products(f, psi, q)
-    send_pieces(di, di_recv, j, along_column)
-    send_elementals(1)
     from_left(f.at[0], 0, q, x)
-    send_pieces(df, df_recv, k, along_row)
     from_left(f.at[1], 1, q, x)
+    spread_and_pair(di, di_recv, j, in_column)
+    spread_and_pair(df, df_recv, k, in_row)
     receive_elementals(0)
     box_products(c, 0, phi, x, p, pt)
     receive_shared(0)
     box_products(twin, 0, phi, x, p, pt)
-    receive(di, di_recv, j)
-    from_left(di, 0, q, r)
-    from_left(di, 1, q, r)
-    loop_products(0, g, r, y)
+    spread(di, di_recv, j, pair(j), in_column)
+    spread(df, df_recv, k, pair(k), in_row)
     receive_elementals(1)
-    loop_products(1, g, r, y)
     box_products(c, 1, phi, x, p, pt)
     sink_transposes(c, phi, phit)
-    receive(df, df_recv, k)
-    sink_products(c, phi, phit, df, st, zt)
-    z_copy = remote(zt.at[c], zt.at[c], z_send, z_recv, sibling)
-    z_copy.start()
     receive_shared(1)
     box_products(twin, 1, phi, x, p, pt)
     sink_transposes(twin, phi, phit)
     box_traces(c, op, p, pt, out)
     box_traces(twin, op, p, pt, out)
+    for step in (1, 3, 2):
+        arrive(di, di_recv, across(j, step))
+        arrive(di, di_recv, across(pair(j), step))
+    from_left(di, 0, q, r)
+    from_left(di, 1, q, r)
+    loop_products(0, g, r, y)
+    loop_products(1, g, r, y)
+    for step in (1, 3, 2):
+        arrive(df, df_recv, across(k, step))
+        arrive(df, df_recv, across(pair(k), step))
+    sink_products(c, phi, phit, df, st, zt, lambda a: hand(a).start())
     loop_traces(c, op, zt, phit, y, out)
-    wait_for(zt.at[twin], z_recv)
+    for a in range(2):
+        wait_for(zt.at[twin, pl.ds(2 * a, 2)], z_recv.at[a])
     loop_traces(twin, op, zt, phit, y, out)
 
     for step in range(1, 8):
-        for copy in (sinks(0, step), sinks(1, step), along_column(step), along_row(step)):
+        for copy in (sinks(0, step), sinks(1, step)):
             copy.wait_send()
-    for copy in (share(0), share(1), z_copy):
+    for copy in sent + [share(0), share(1), hand(0), hand(1)]:
         copy.wait_send()
 
     @pl.when(j == k)
@@ -362,8 +393,8 @@
             pltpu.VMEM((2, 2, N, W), BF),
             pltpu.VMEM((2, N, W), BF),
             pltpu.VMEM((2, 4, N, W), BF),
-            sems((2, 8)), sems((2, 8)), sems((8,)), sems((8,)), sems((8,)), sems((8,)), sems((16,)),
-            sems((2,)), sems((2,)), sems, sems, sems((2,)),
+            sems((2, 8)), sems((2, 8)), sems((8,)), sems((8,)), sems((16,)), sems((16,)),
+            sems((2,)), sems((2,)), sems((2,)), sems((2,)), sems((2,)),
         ],
         compiler_params=pltpu.CompilerParams(
             collective_id=0, has_side_effects=True, vmem_limit_bytes=60 * 2**20),

time: 65.3 us -> 60.1 us (0.920)
  the two profiles are of different devices: /device:TPU:22 before, /device:TPU:1 now
where the time goes in v3:
time: 60.1 us; the launch traced here: 59.9 us
  Pallas kernels  58.6 us (98%)
  local copies, waits for them, and re-layouts  1.35 us (2%)
    pallas_call x1, Pallas kernels, on_device(): pl.pallas_call(kernel, out_shape=jax.ShapeDtypeStruct((2, 1, 3, 2, 4, 4),...  58.6 us
    unnamed x1, local copies, waits for them, and re-layouts  1.35 us

profile of v3, /device:TPU:1, one launch (start us, length us, event | category | flops | bytes accessed | tf_op | source)
XLA Modules:
  0.0 59.9 jit_solution(2268846027413208429)
XLA Ops:
  0.0 58.6 %shard_map.37 = f32[2,1,3,2,4,4]{5,4,3,2,1,0:T(4,128)} custom-call(s32[2,4]{1,0:T(2,128)} %bitcast.5, bf16[2,8,96,384]{3,2,1,0:T(8,128)(2,1)} %bitcast.3, bf16[2,8,96,384]{3,2,1,0:T(8,128)(2,1)} %bitcast.4), custom_call_target="tpu_custom_call" | custom-call | flops 20000000000 | bytes 4000000 | tf_op jit(solution)/shard_map/pallas_call | solution.py:375
  58.6 1.3 %copy.5 = f32[2,1,3,2,4,4]{5,4,3,2,1,0:T(4,128)} copy(f32[2,1,3,2,4,4]{5,4,3,2,1,0:T(4,128)} %shard_map.37) | data formatting | bytes 1536

commit v4 on v3

--- a/solution.py
+++ b/solution.py
@@ -325,16 +325,20 @@
     box_products(c, 0, phi, x, p, pt)
     receive_shared(0)
     box_products(twin, 0, phi, x, p, pt)
-    spread(di, di_recv, j, pair(j), in_column)
-    spread(df, df_recv, k, pair(k), in_row)
     receive_elementals(1)
     box_products(c, 1, phi, x, p, pt)
     sink_transposes(c, phi, phit)
+    spread(di, di_recv, j, pair(j), in_column)
+    spread(df, df_recv, k, pair(k), in_row)
     receive_shared(1)
     box_products(twin, 1, phi, x, p, pt)
     sink_transposes(twin, phi, phit)
     box_traces(c, op, p, pt, out)
     box_traces(twin, op, p, pt, out)
+    for step in (1, 3, 2):
+        arrive(df, df_recv, across(k, step))
+        arrive(df, df_recv, across(pair(k), step))
+    sink_products(c, phi, phit, df, st, zt, lambda a: hand(a).start())
     for step in (1, 3, 2):
         arrive(di, di_recv, across(j, step))
         arrive(di, di_recv, across(pair(j), step))
@@ -342,10 +346,6 @@
     from_left(di, 1, q, r)
     loop_products(0, g, r, y)
     loop_products(1, g, r, y)
-    for step in (1, 3, 2):
-        arrive(df, df_recv, across(k, step))
-        arrive(df, df_recv, across(pair(k), step))
-    sink_products(c, phi, phit, df, st, zt, lambda a: hand(a).start())
     loop_traces(c, op, zt, phit, y, out)
     for a in range(2):
         wait_for(zt.at[twin, pl.ds(2 * a, 2)], z_recv.at[a])

time: 60.1 us -> 58.9 us (0.980)
  the two profiles are of different devices: /device:TPU:1 before, /device:TPU:0 now
where the time goes in v4:
time: 58.9 us; the launch traced here: 58.7 us
  Pallas kernels  57.4 us (97%)
  local copies, waits for them, and re-layouts  1.35 us (2%)
    pallas_call x1, Pallas kernels, on_device(): pl.pallas_call(kernel, out_shape=jax.ShapeDtypeStruct((2, 1, 3, 2, 4, 4),...  57.4 us
    unnamed x1, local copies, waits for them, and re-layouts  1.35 us

profile of v4, /device:TPU:0, one launch (start us, length us, event | category | flops | bytes accessed | tf_op | source)
XLA Modules:
  0.0 58.7 jit_solution(200808634942172184)
XLA Ops:
  0.0 57.4 %shard_map.37 = f32[2,1,3,2,4,4]{5,4,3,2,1,0:T(4,128)} custom-call(s32[2,4]{1,0:T(2,128)} %bitcast.5, bf16[2,8,96,384]{3,2,1,0:T(8,128)(2,1)} %bitcast.3, bf16[2,8,96,384]{3,2,1,0:T(8,128)(2,1)} %bitcast.4), custom_call_target="tpu_custom_call" | custom-call | flops 20000000000 | bytes 4000000 | tf_op jit(solution)/shard_map/pallas_call | solution.py:375
  57.4 1.3 %copy.5 = f32[2,1,3,2,4,4]{5,4,3,2,1,0:T(4,128)} copy(f32[2,1,3,2,4,4]{5,4,3,2,1,0:T(4,128)} %shard_map.37) | data formatting | bytes 1536

commit v5 on v4

--- a/solution.py
+++ b/solution.py
@@ -328,8 +328,8 @@
     receive_elementals(1)
     box_products(c, 1, phi, x, p, pt)
     sink_transposes(c, phi, phit)
+    spread(df, df_recv, k, pair(k), in_row)
     spread(di, di_recv, j, pair(j), in_column)
-    spread(df, df_recv, k, pair(k), in_row)
     receive_shared(1)
     box_products(twin, 1, phi, x, p, pt)
     sink_transposes(twin, phi, phit)

time: 58.9 us -> 58 us (0.985); the launches traced: 58.7 us -> 57.1 us
  Pallas kernels: 57.4 us -> 55.7 us
    pallas_call x1, Pallas kernels: 57.4 us -> 55.7 us  [on_device(): pl.pallas_call(kernel, out_shape=jax.ShapeDtypeStruct((2, 1, 3, 2, 4, 4),...]
where the time goes in v5:
time: 58 us; the launch traced here: 57.1 us
  Pallas kernels  55.7 us (96%)
  local copies, waits for them, and re-layouts  1.35 us (2%)
    pallas_call x1, Pallas kernels, on_device(): pl.pallas_call(kernel, out_shape=jax.ShapeDtypeStruct((2, 1, 3, 2, 4, 4),...  55.7 us
    unnamed x1, local copies, waits for them, and re-layouts  1.35 us

profile of v5, /device:TPU:0, one launch (start us, length us, event | category | flops | bytes accessed | tf_op | source)
XLA Modules:
  0.0 57.1 jit_solution(3238097072288783862)
XLA Ops:
  0.0 55.7 %shard_map.37 = f32[2,1,3,2,4,4]{5,4,3,2,1,0:T(4,128)} custom-call(s32[2,4]{1,0:T(2,128)} %bitcast.5, bf16[2,8,96,384]{3,2,1,0:T(8,128)(2,1)} %bitcast.3, bf16[2,8,96,384]{3,2,1,0:T(8,128)(2,1)} %bitcast.4), custom_call_target="tpu_custom_call" | custom-call | flops 20000000000 | bytes 4000000 | tf_op jit(solution)/shard_map/pallas_call | solution.py:375
  55.7 1.3 %copy.5 = f32[2,1,3,2,4,4]{5,4,3,2,1,0:T(4,128)} copy(f32[2,1,3,2,4,4]{5,4,3,2,1,0:T(4,128)} %shard_map.37) | data formatting | bytes 1536
